TPU v7x, 32 devices: a whole 2x2x4 slice. The times are simulated.
32 devices in a mesh: tok: 8 (over y, x, core), ch: 4 (over z).
Axes of the slice: x: 2, y: 2, z: 4, core: 2. Of those that a mesh axis runs over, the one named last changes fastest.
Arguments:
- activations: bfloat16 [2048, 8192], P('tok', 'ch'), may hold values from -25 to 25
- weight: bfloat16 [14336, 8192], P('tok', 'ch'), may hold values from -0.0625 to 0.0625
- basis: bfloat16 [1024, 8192], P(None, 'ch'), may hold values from -0.0625 to 0.0625
Outputs:
- left_factor: float32 [14336, 1024], P(('tok', 'ch'))
All inputs are finite; a program needn't handle non-finite values.
Results may differ from a plain program's by a relative error of at most 0.0088.
Values sent between devices are 32-bit elements; how exact they have to be, the bound alone decides.
A program may use at most 128 MiB of HBM per device.

v0:
```python
import jax
import jax.numpy as jnp
from jax import lax
from jax.sharding import PartitionSpec as P

damping = 0.1


def shards(activations, weight, basis):
    partial_value = lax.dot_general(
        activations, basis, (((1,), (1,)), ((), ())), preferred_element_type=jnp.float32
    )
    codes = lax.psum(partial_value, "ch")
    rank_width = codes.shape[1]
    channels = lax.axis_size("ch")
    column_width = rank_width // channels
    own_columns = lax.dynamic_slice_in_dim(
        codes, lax.axis_index("ch") * column_width, column_width, 1
    )
    columns = lax.dot_general(
        codes,
        own_columns,
        (((0,), (0,)), ((), ())),
        precision=lax.Precision.HIGHEST,
        preferred_element_type=jnp.float32,
    )
    summed = lax.psum(columns, "tok")
    gram = lax.all_gather(summed, "ch", axis=1, tiled=True)
    codes_low = codes.astype(jnp.bfloat16)
    local_moments = lax.dot_general(
        activations, codes_low, (((0,), (0,)), ((), ())), preferred_element_type=jnp.float32
    )
    moments = lax.psum(local_moments, "tok")
    rows_part = weight.astype(jnp.float32)
    cross = lax.psum_scatter(
        jnp.dot(
            rows_part, moments, precision=lax.Precision.HIGHEST, preferred_element_type=jnp.float32
        ),
        "ch",
        scatter_dimension=0,
        tiled=True,
    )
    ridge = damping * jnp.trace(gram) / rank_width
    damped = gram + ridge * jnp.eye(rank_width, dtype=jnp.float32)
    lower = jnp.linalg.cholesky(damped)
    middle = jax.scipy.linalg.solve_triangular(lower, cross.T, lower=True)
    solved = jax.scipy.linalg.solve_triangular(lower, middle, trans=1, lower=True)
    return solved.T


def solution(mesh):
    in_specs = (P("tok", "ch"), P("tok", "ch"), P(None, "ch"))
    out_specs = P(("tok", "ch"), None)
    return jax.shard_map(shards, mesh=mesh, in_specs=in_specs, out_specs=out_specs, check_vma=False)
```

profile of v0, /device:TPU:0, one launch (start us, length us, event | category | flops | bytes accessed | tf_op | source)
XLA Modules:
  0.0 666.6 jit_solution(14302103406288494500)
XLA Ops:
  6.5 1.2 copy-done
  7.8 4.4 fusion.99
  12.3 54.6 %all-reduce.5.cloned.1.call-done = f32[256,1024]{1,0:T(8,128)} async-done(((f32[256,1024]{1,0:T(8,128)}), f32[256,1024]{1,0:T(8,128)}) %all-reduce.5.cloned.1.call-update) | async-done | bytes 1048592 | tf_op jit(solution)/shard_map/psum | solution.py:13
  66.9 5.8 convolution_bitcast_fusion.1
  72.7 2.1 fusion.56
  74.9 137.7 %all-reduce.7.cloned.1.call-done = (f32[2048,1024]{0,1:T(8,128)}, f32[1024,256]{0,1:T(8,128)}) async-done(((f32[2048,1024]{0,1:T(8,128)}, f32[1024,256]{0,1:T(8,128)}), (f32[2048,1024]{0,1:T(8,128)}, f32[1024,256]{0,1:T(8,128)})) %all-reduce.7.cloned.1.call-update) | async-done | bytes 9437200 | tf_op jit(solution)/shard_map/psum | solution.py:33
  212.9 29.9 %convolution_bitcast_fusion = f32[1792,1024]{0,1:T(8,128)} fusion(f32[2048,1024]{0,1:T(8,128)} %get-tuple-element.29, bf16[1792,2048]{1,0:T(8,128)(2,1)} %param.4), kind=kOutput, calls=%fused_computation.3 | convolution fusion | flops 45097156608 | bytes 23068672 | tf_op jit(solution)/shard_map/dot_general | solution.py:36
  242.8 8.4 %copy.47 = f32[1792,1024]{1,0:T(8,128)} copy(f32[1792,1024]{0,1:T(8,128)} %convolution_bitcast_fusion) | data formatting | bytes 14680064
  251.3 43.8 %all-gather.2.cloned.1.call-done = f32[1024,1024]{0,1:T(8,128)} async-done(((f32[1024,256]{0,1:T(8,128)}), f32[1024,1024]{0,1:T(8,128)}) %all-gather.2.cloned.1.call-update) | async-done | bytes 4194320 | tf_op jit(solution)/shard_map/all_gather | solution.py:28
  295.1 2.9 select_reduce_fusion
  298.6 5.1 select_add_fusion
  303.8 5.8 copy.23
  309.6 4.5 fusion
  314.1 2.1 copy-done.4
  316.2 11.7 %cholesky.222 = f32[128,128]{1,0:T(8,128)S(1)} custom-call(f32[128,128]{1,0:T(8,128)S(1)} %cholesky.577), custom_call_target="Cholesky" | custom-call | tf_op jit(solution)/shard_map/jit(cholesky)/cholesky | solution.py:45
  328.0 9.8 %custom-call.66 = f32[1,128,128]{1,2,0:T(8,128)S(1)} custom-call(f32[1,128,128]{2,1,0:T(8,128)S(1)} %get-tuple-element.63), custom_call_target="InvertDiagBlocksLowerTriangular" | custom-call | tf_op jit(solution)/shard_map/jit(cholesky)/cholesky | solution.py:45
  337.8 1.5 fusion.34
  339.6 1.6 convolution_subtract_fusion
  341.1 11.7 %cholesky.243 = f32[128,128]{1,0:T(8,128)S(1)} custom-call(f32[128,128]{1,0:T(8,128)S(1)} %cholesky.581), custom_call_target="Cholesky" | custom-call | tf_op jit(solution)/shard_map/jit(cholesky)/cholesky | solution.py:45
  353.1 9.8 %custom-call.67 = f32[1,128,128]{1,2,0:T(8,128)S(1)} custom-call(f32[1,128,128]{2,1,0:T(8,128)S(1)} %get-tuple-element.61), custom_call_target="InvertDiagBlocksLowerTriangular" | custom-call | tf_op jit(solution)/shard_map/jit(cholesky)/cholesky | solution.py:45
  364.1 2.0 copy-done.2
  366.1 2.4 convolution_subtract_fusion.1
  368.5 11.7 %cholesky.466 = f32[128,128]{1,0:T(8,128)S(1)} custom-call(f32[128,128]{1,0:T(8,128)S(1)} %cholesky.586), custom_call_target="Cholesky" | custom-call | tf_op jit(solution)/shard_map/jit(cholesky)/cholesky | solution.py:45
  380.4 9.8 %custom-call.68 = f32[1,128,128]{1,2,0:T(8,128)S(1)} custom-call(f32[1,128,128]{2,1,0:T(8,128)S(1)} %get-tuple-element.59), custom_call_target="InvertDiagBlocksLowerTriangular" | custom-call | tf_op jit(solution)/shard_map/jit(cholesky)/cholesky | solution.py:45
  390.9 1.3 convolution_dynamic-update-slice_fusion.1
  392.1 3.3 convolution_subtract_fusion.2
  395.5 11.7 %cholesky.485 = f32[128,128]{1,0:T(8,128)S(1)} custom-call(f32[128,128]{1,0:T(8,128)S(1)} %cholesky.591), custom_call_target="Cholesky" | custom-call | tf_op jit(solution)/shard_map/jit(cholesky)/cholesky | solution.py:45
  407.3 9.8 %custom-call.69 = f32[1,128,128]{1,2,0:T(8,128)S(1)} custom-call(f32[1,128,128]{2,1,0:T(8,128)S(1)} %get-tuple-element.57), custom_call_target="InvertDiagBlocksLowerTriangular" | custom-call | tf_op jit(solution)/shard_map/jit(cholesky)/cholesky | solution.py:45
  417.8 1.1 convolution_dynamic-update-slice_fusion.2
  418.9 3.1 convolution_subtract_fusion.10
  422.1 12.2 %cholesky.504 = f32[128,128]{1,0:T(8,128)S(1)} custom-call(f32[128,128]{1,0:T(8,128)S(1)} %cholesky.596), custom_call_target="Cholesky" | custom-call | tf_op jit(solution)/shard_map/jit(cholesky)/cholesky | solution.py:45
  434.4 9.8 %custom-call.70 = f32[1,128,128]{1,2,0:T(8,128)S(1)} custom-call(f32[1,128,128]{2,1,0:T(8,128)S(1)} %get-tuple-element.55), custom_call_target="InvertDiagBlocksLowerTriangular" | custom-call | tf_op jit(solution)/shard_map/jit(cholesky)/cholesky | solution.py:45
  444.9 1.1 convolution_dynamic-update-slice_fusion.4
  446.0 3.1 convolution_subtract_fusion.18
  449.1 11.7 %cholesky.524 = f32[128,128]{1,0:T(8,128)S(1)} custom-call(f32[128,128]{1,0:T(8,128)S(1)} %cholesky.601), custom_call_target="Cholesky" | custom-call | tf_op jit(solution)/shard_map/jit(cholesky)/cholesky | solution.py:45
  461.0 9.8 %custom-call.71 = f32[1,128,128]{1,2,0:T(8,128)S(1)} custom-call(f32[1,128,128]{2,1,0:T(8,128)S(1)} %get-tuple-element.53), custom_call_target="InvertDiagBlocksLowerTriangular" | custom-call | tf_op jit(solution)/shard_map/jit(cholesky)/cholesky | solution.py:45
  472.4 2.8 convolution_subtract_fusion.19
  475.3 11.7 %cholesky.544 = f32[128,128]{1,0:T(8,128)S(1)} custom-call(f32[128,128]{1,0:T(8,128)S(1)} %cholesky.606), custom_call_target="Cholesky" | custom-call | tf_op jit(solution)/shard_map/jit(cholesky)/cholesky | solution.py:45
  487.1 9.8 %custom-call.72 = f32[1,128,128]{1,2,0:T(8,128)S(1)} custom-call(f32[1,128,128]{2,1,0:T(8,128)S(1)} %get-tuple-element.51), custom_call_target="InvertDiagBlocksLowerTriangular" | custom-call | tf_op jit(solution)/shard_map/jit(cholesky)/cholesky | solution.py:45
  498.6 2.1 convolution_subtract_fusion.20
  500.6 11.7 %cholesky.562 = f32[128,128]{1,0:T(8,128)S(1)} custom-call(f32[128,128]{1,0:T(8,128)S(1)} %convolution_subtract_fusion.20), custom_call_target="Cholesky" | custom-call | tf_op jit(solution)/shard_map/jit(cholesky)/cholesky | solution.py:45
  522.8 5.0 select_select_fusion
  527.8 24.3 %while.1 = (s32[]{:T(128)}, f32[1024,1024]{0,1:T(8,128)}, s32[8,2]{0,1:T(2,128)S(1)}, f32[8,128,128]{2,1,0:T(8,128)S(1)}, s32[]{:T(128)}) while((s32[]{:T(128)}, f32[1024,1024]{0,1:T(8,128)}, s32[8,2]{0,1:T(2,128)S(1)}, f32[8,128,128]{2,1,0:T(8,128)S(1)}, s32[]{:T(128)}) %tuple.50), condition=%wide.while_cond, body=%wide.while_body.sunk | while | flops 2 | bytes 393329 | solution.py:47
  528.5 2.3 dynamic-slice.7
  531.5 2.3 dynamic-slice.7
  534.6 2.3 dynamic-slice.7
  537.6 2.3 dynamic-slice.7
  540.7 2.3 dynamic-slice.7
  543.7 2.3 dynamic-slice.7
  546.7 2.3 dynamic-slice.7
  549.8 2.2 dynamic-slice.7
  552.1 78.6 %custom-call.73 = f32[8,128,128]{1,2,0:T(8,128)S(1)} custom-call(f32[8,128,128]{2,1,0:T(8,128)S(1)} %get-tuple-element.12), custom_call_target="InvertDiagBlocksLowerTriangular" | custom-call | tf_op jit(solution)/shard_map/jit(_solve_triangular)/triangular_solve | solution.py:47
  630.8 2.3 copy.48
  633.6 1.4 convolution_subtract_fusion.7
  635.7 1.5 convolution_subtract_fusion.6
  639.2 1.1 convolution_subtract_fusion.9
  640.9 1.3 convolution_subtract_fusion.4
  642.8 1.5 convolution_subtract_fusion.3
  644.9 1.8 convolution_subtract_fusion.8
  652.1 1.1 convolution_subtract_fusion.12
  653.7 1.2 convolution_subtract_fusion.11
  655.4 1.5 convolution_subtract_fusion.16
  656.9 1.2 convolution_dynamic-update-slice_fusion.3
  658.4 1.2 copy-done.7
  (141 shorter events, 30.5 us)
Async XLA Ops:
  6.5 1.2 copy-start
  6.5 60.4 %all-reduce.5.cloned.1.call-start = ((), (), s32[]{:S(2)}) async-start(), calls=%async_computation.1 | async-start | bytes 2097152 | tf_op jit(solution)/shard_map/psum | solution.py:13
  12.2 200.4 %all-reduce.7.cloned.1.call-start = ((), (), s32[]{:S(2)}) async-start(), calls=%async_computation.4 | async-start | bytes 18874368 | tf_op jit(solution)/shard_map/psum | solution.py:33
  66.9 5.8 copy-start.5
  74.8 220.2 %all-gather.2.cloned.1.call-start = ((), (), s32[]{:S(2)}) async-start(), calls=%async_computation.2 | async-start | bytes 5242880 | tf_op jit(solution)/shard_map/all_gather | solution.py:28
  212.6 418.1 %reduce-scatter.4.cloned.1.call-start = ((), (), s32[]{:S(2)}) async-start(), calls=%async_computation.3 | async-start | bytes 9175040
  314.1 2.1 copy-start.4
  364.1 2.0 copy-start.2
  630.7 24.2 %copy-start.6 = (f32[8,128,128]{1,2,0:T(8,128)}, f32[8,128,128]{1,2,0:T(8,128)S(1)}, u32[]{:S(2)}) copy-start(f32[8,128,128]{1,2,0:T(8,128)S(1)} %custom-call.73) | copy-start | bytes 1572868
  633.6 4.2 copy-start.3
  655.4 4.1 copy-start.1
  658.3 1.2 copy-start.7
Sparse Core Ops, SparseCore 0:
  12.3 54.5 all-reduce.4
  74.9 137.6 all-reduce.6
  214.2 80.8 all-gather.1
  297.2 126.2 reduce-scatter.3
where the time goes:
time: 671 us; the launch traced here: 667 us
  other arithmetic  264 us (39%)
  waiting for transfers between devices  236 us (35%)
  matrix products  92.7 us (14%)
  local copies, waits for them, and re-layouts  53.1 us (8%)
  between operations  20.2 us (3%)
    another operation x30, other arithmetic, shards(): lower = jnp.linalg.cholesky(damped)  168 us
    psum x1, waiting for transfers between devices, shards(): moments = lax.psum(local_moments, 'tok')  138 us
    another operation x3, other arithmetic, shards(): jax.scipy.linalg.solve_triangular(lower, middle, trans=1, lower=True)  83.6 us
    psum x1, waiting for transfers between devices, shards(): codes = lax.psum(partial_value, 'ch')  54.6 us
    all_gather x1, waiting for transfers between devices, shards(): gram = lax.all_gather(summed, 'ch', axis=1, tiled=True)  43.8 us
    dot_general x1, matrix products, shards(): jnp.dot(rows_part, moments, precision=lax.Precision.HIGHEST, preferred_el...  29.9 us
    another operation x14, matrix products, shards(): lower = jnp.linalg.cholesky(damped)  26 us
    another operation x40, local copies, waits for them, and re-layouts  24 us
  transfers between devices with their start and end apart: 4, of which 3 were waited for; matrix products, arithmetic and copies ran while one was open for 55% of the time, Pallas kernels for 0%

commit v1 on v0

v1 whole, which is shorter than its diff:
```python
import jax
import jax.numpy as jnp
from jax import lax
from jax.experimental import pallas as pl
from jax.experimental.pallas import tpu as pltpu
from jax.sharding import PartitionSpec as P

damping = 0.1
block = 128
group = 4
HIGHEST = lax.Precision.HIGHEST


def dot_f32(a, b, dims=(((1,), (0,)), ((), ()))):
    return lax.dot_general(a, b, dims, precision=HIGHEST, preferred_element_type=jnp.float32)


NT = (((1,), (1,)), ((), ()))


def factor_inverse(a):
    n = a.shape[0]
    tiles = n // 8
    lanes = lax.broadcasted_iota(jnp.int32, (8, n), 1)
    subs = lax.broadcasted_iota(jnp.int32, (8, n), 0)
    left = [a[8 * t : 8 * t + 8] for t in range(tiles)]
    right = [(lanes == subs + 8 * t).astype(jnp.float32) for t in range(tiles)]
    for start in range(0, n, group):
        first = start // 8
        base = start - 8 * first
        rows = [
            (left[first][base + g : base + g + 1], right[first][base + g : base + g + 1])
            for g in range(group)
        ]
        cols = {
            t: [
                jnp.broadcast_to(left[t][:, start + g : start + g + 1], (8, n))
                for g in range(group)
            ]
            for t in range(first, tiles)
        }
        small = [
            [cols[first][h][base + g : base + g + 1] for h in range(group)] for g in range(group)
        ]
        inverse = []
        factors = [[None] * group for _ in range(group)]
        for g in range(group):
            inverse.append(1.0 / small[g][g])
            for h in range(g + 1, group):
                f = small[h][g] * inverse[g]
                factors[h][g] = f
                for k in range(g + 1, group):
                    small[h][k] = small[h][k] - f * small[g][k]
                rows[h] = (rows[h][0] - f * rows[g][0], rows[h][1] - f * rows[g][1])
        scaled = [small[g] for g in range(group)]
        for t in range(first, tiles):
            mults = []
            for g in range(group):
                c = cols[t][g]
                for k in range(g):
                    c = c - mults[k] * scaled[k][g]
                m = c * inverse[g]
                if t == first:
                    m = jnp.where(subs > base + g, m, 0.0)
                mults.append(m)
            for g in range(group):
                left[t] = left[t] - mults[g] * rows[g][0]
                right[t] = right[t] - mults[g] * rows[g][1]
    out = []
    for t in range(tiles):
        pivot = jnp.sum(
            jnp.where(lanes == subs + 8 * t, left[t], 0.0), axis=1, keepdims=True
        )
        out.append(right[t] * (1.0 / jnp.sqrt(pivot)))
    return jnp.concatenate(out, axis=0)


def inverse_factor_kernel(gram_ref, out_ref, work, diag):
    n = gram_ref.shape[0]
    steps = n // block
    trace = jnp.zeros((1, 1), jnp.float32)
    eye = lax.broadcasted_iota(jnp.int32, (block, block), 0) == lax.broadcasted_iota(
        jnp.int32, (block, block), 1
    )
    for k in range(steps):
        s = slice(k * block, (k + 1) * block)
        trace += jnp.sum(jnp.where(eye, gram_ref[s, s], 0.0), keepdims=True)
    ridge = damping * trace / n
    work[...] = gram_ref[...]
    for k in range(steps):
        s = slice(k * block, (k + 1) * block)
        work[s, s] = gram_ref[s, s] + jnp.where(eye, ridge, 0.0)

    def step(k, carry):
        o = pl.multiple_of(k * block, block)
        diag[...] = factor_inverse(work[pl.ds(o, block), pl.ds(o, block)])
        for kk in range(steps):

            @pl.when(k == kk)
            def _(kk=kk):
                s = slice(kk * block, (kk + 1) * block)
                inv = diag[...]
                row = dot_f32(inv, work[s, :])
                work[s, :] = row
                work[s, s] = inv
                row = work[s, :]
                for t in range(kk + 1, steps):
                    r = slice(t * block, (t + 1) * block)
                    mult = dot_f32(work[r, s], inv, NT)
                    work[r, s] = jnp.zeros((block, block), jnp.float32)
                    work[r, :] = work[r, :] - dot_f32(mult, row)

        return carry

    lax.fori_loop(0, steps, step, 0)
    for k in range(steps):
        s = slice(k * block, (k + 1) * block)
        if k:
            out_ref[s, : k * block] = work[s, : k * block]
        out_ref[s, s] = work[s, s]
        if k + 1 < steps:
            out_ref[s, (k + 1) * block :] = jnp.zeros((block, n - (k + 1) * block), jnp.float32)


def inverse_factor(gram):
    n = gram.shape[0]
    return pl.pallas_call(
        inverse_factor_kernel,
        out_shape=jax.ShapeDtypeStruct((n, n), jnp.float32),
        in_specs=[pl.BlockSpec(memory_space=pltpu.VMEM)],
        out_specs=pl.BlockSpec(memory_space=pltpu.VMEM),
        scratch_shapes=[
            pltpu.VMEM((n, n), jnp.float32),
            pltpu.VMEM((block, block), jnp.float32),
        ],
        compiler_params=pltpu.CompilerParams(vmem_limit_bytes=32 * 1024 * 1024),
        cost_estimate=pl.CostEstimate(
            flops=100_000_000_000, bytes_accessed=8 * n * n, transcendentals=0
        ),
        name="inverse_factor",
    )(gram)


def shards(activations, weight, basis):
    partial_value = lax.dot_general(
        activations, basis, (((1,), (1,)), ((), ())), preferred_element_type=jnp.float32
    )
    codes = lax.psum(partial_value, "ch")
    local_gram = dot_f32(codes, codes, (((0,), (0,)), ((), ())))
    gram = lax.psum(local_gram, "tok")
    codes_low = codes.astype(jnp.bfloat16)
    local_moments = lax.dot_general(
        activations, codes_low, (((0,), (0,)), ((), ())), preferred_element_type=jnp.float32
    )
    gram, local_moments = lax.optimization_barrier((gram, local_moments))
    inverse = inverse_factor(gram)
    moments = lax.psum(local_moments, "tok")
    high = lax.reduce_precision(moments, 8, 7)
    rest = (moments - high).astype(jnp.bfloat16)
    high = high.astype(jnp.bfloat16)
    cross = lax.psum_scatter(
        jnp.dot(weight, high, preferred_element_type=jnp.float32)
        + jnp.dot(weight, rest, preferred_element_type=jnp.float32),
        "ch",
        scatter_dimension=0,
        tiled=True,
    )
    middle = lax.dot_general(
        cross, inverse, NT, precision=lax.Precision.HIGH, preferred_element_type=jnp.float32
    )
    return jnp.dot(
        middle, inverse, precision=lax.Precision.HIGH, preferred_element_type=jnp.float32
    )


def solution(mesh):
    in_specs = (P("tok", "ch"), P("tok", "ch"), P(None, "ch"))
    out_specs = P(("tok", "ch"), None)
    return jax.shard_map(shards, mesh=mesh, in_specs=in_specs, out_specs=out_specs, check_vma=False)
```

time: 671 us -> 472 us (0.70)
  other arithmetic: 264 us -> 0 us
  waiting for transfers between devices: 236 us -> 321 us
  Pallas kernels: 0 us -> 63 us
  local copies, waits for them, and re-layouts: 53.1 us -> 13.9 us
  matrix products: 92.7 us -> 54.6 us
    another operation x33 -> x0, other arithmetic: 251 us -> none  [the longest x30 168 us: shards(): lower = jnp.linalg.cholesky(damped)]
    psum x0 -> x1, waiting for transfers between devices: none -> 76 us  [shards(): gram = lax.psum(local_gram, 'tok')]
    pallas_call x0 -> x1, Pallas kernels: none -> 63 us  [inverse_factor(): pl.pallas_call(inverse_factor_kernel, out_shape=jax.ShapeDtypeStruct((n,...]
    unnamed x5, waiting for transfers between devices: 0.09 us -> 60.9 us
    another operation x44 -> x0, matrix products: 50.4 us -> none  [the longest x14 26 us: shards(): lower = jnp.linalg.cholesky(damped)]
    all_gather x1 -> x0, waiting for transfers between devices: 43.8 us -> none  [shards(): gram = lax.all_gather(summed, 'ch', axis=1, tiled=True)]
    another operation x70 -> x0, local copies, waits for them, and re-layouts: 29.7 us -> none
    dot_general x2 -> x5, matrix products: 32 us -> 45.6 us  [the longest x1 14.3 us: shards(): jnp.dot(weight, rest, preferred_element_type=jnp.float32)]
  transfers between devices with their start and end apart: 4 -> 4, of which waited for: 3 -> 4; matrix products, arithmetic and copies ran while one was open for 55% -> 1% of each run, Pallas kernels for 0% -> 13%
where the time goes in v1:
time: 472 us; the launch traced here: 467 us
  waiting for transfers between devices  321 us (68%)
  Pallas kernels  63 us (13%)
  matrix products  54.6 us (12%)
  local copies, waits for them, and re-layouts  13.9 us (3%)
  between operations  13.6 us (3%)
    psum x1, waiting for transfers between devices, shards(): moments = lax.psum(local_moments, 'tok')  130 us
    psum x1, waiting for transfers between devices, shards(): gram = lax.psum(local_gram, 'tok')  76 us
    pallas_call x1, Pallas kernels, inverse_factor(): pl.pallas_call(inverse_factor_kernel, out_shape=jax.ShapeDtypeStruct((n,...  63 us
    unnamed x5, waiting for transfers between devices  60.9 us
    psum x1, waiting for transfers between devices, shards(): codes = lax.psum(partial_value, 'ch')  54.6 us
    dot_general x1, matrix products, shards(): jnp.dot(weight, rest, preferred_element_type=jnp.float32)  14.3 us
    unnamed x15, local copies, waits for them, and re-layouts  13.9 us
    dot_general x1, matrix products, shards(): jnp.dot(weight, high, preferred_element_type=jnp.float32)  13.7 us
  transfers between devices with their start and end apart: 4, of which 4 were waited for; matrix products, arithmetic and copies ran while one was open for 1% of the time, Pallas kernels for 13%

profile of v1, /device:TPU:0, one launch (start us, length us, event | category | flops | bytes accessed | tf_op | source)
XLA Modules:
  0.0 466.8 jit_solution(6348483753708421347)
XLA Ops:
  6.5 0.0 copy-start
  6.5 0.0 all-reduce.4.cloned.1.call-start
  6.5 1.2 copy-done
  7.8 4.4 fusion.5
  12.2 0.0 all-reduce.4.cloned.1.call-update
  12.2 0.0 all-reduce.6.cloned.1.call-start
  12.3 54.6 %all-reduce.4.cloned.1.call-done = f32[256,1024]{1,0:T(8,128)} async-done(((f32[256,1024]{1,0:T(8,128)}), f32[256,1024]{1,0:T(8,128)}) %all-reduce.4.cloned.1.call-update) | async-done | bytes 1048592 | tf_op jit(solution)/shard_map/psum | solution.py:148
  66.9 0.0 copy-start.5
  66.9 7.1 %fusion.6 = f32[1024,1024]{1,0:T(8,128)} fusion(f32[256,1024]{1,0:T(8,128)} %all-reduce.4.cloned.1.call-done), kind=kOutput, calls=%fused_computation.9 | convolution fusion | flops 3221225472 | bytes 5242880 | tf_op jit(solution)/shard_map/dot_general | solution.py:15
  74.0 0.0 all-reduce.6.cloned.1.call-update
  74.0 0.0 all-reduce.8.cloned.1.call-start
  74.1 0.0 copy-done.5
  74.1 4.5 convolution_bitcast_fusion
  78.6 76.0 %all-reduce.6.cloned.1.call-done.gram_ref = f32[1024,1024]{1,0:T(8,128)} async-done(((f32[1024,1024]{1,0:T(8,128)}), f32[1024,1024]{1,0:T(8,128)}) %all-reduce.6.cloned.1.call-update) | async-done | bytes 4194320 | tf_op jit(solution)/shard_map/psum | solution.py:150
  154.6 0.0 all-reduce.8.cloned.1.call-update
  154.6 0.2 reduce-scatter.4.cloned.1.call-start
  154.8 129.9 %all-reduce.8.cloned.1.call-done = f32[2048,1024]{0,1:T(8,128)} async-done(((f32[2048,1024]{0,1:T(8,128)}), f32[2048,1024]{0,1:T(8,128)}) %all-reduce.8.cloned.1.call-update) | async-done | bytes 8388624 | tf_op jit(solution)/shard_map/psum | solution.py:157
  284.7 0.0 copy-start.6
  284.7 14.3 %fusion.1 = f32[1024,1792]{1,0:T(8,128)} fusion(bf16[1792,2048]{1,0:T(8,128)(2,1)} %param.4, f32[2048,1024]{0,1:T(8,128)} %all-reduce.8.cloned.1.call-done), kind=kOutput, calls=%fused_computation.5 | convolution fusion | flops 7522484224 | bytes 23068672 | tf_op jit(solution)/shard_map/dot_general | solution.py:163
  299.0 0.0 copy-done.6
  299.0 13.7 %add_bitcast_fusion = f32[1792,1024]{0,1:T(8,128)} fusion(f32[1024,1792]{1,0:T(8,128)} %fusion.1, bf16[1792,2048]{1,0:T(8,128)(2,1)} %param.4, f32[2048,1024]{0,1:T(8,128)S(1)} %copy-done.6), kind=kOutput, calls=%fused_computation.3 | convolution fusion | flops 7522222080 | bytes 30408704 | tf_op jit(solution)/shard_map/dot_general | solution.py:162
  312.7 8.4 %copy.4 = f32[1792,1024]{1,0:T(8,128)} copy(f32[1792,1024]{0,1:T(8,128)} %add_bitcast_fusion) | data formatting | bytes 14680064
  321.1 0.0 reduce-scatter.4.cloned.1.call-update
  321.2 0.0 copy-start.4
  321.2 2.2 copy-done.4
  323.3 63.0 %inverse_factor.1 = f32[1024,1024]{1,0:T(8,128)S(1)} custom-call(f32[1024,1024]{1,0:T(8,128)S(1)} %copy-done.4), custom_call_target="tpu_custom_call" | custom-call | flops 99999997952 | bytes 8388608 | tf_op jit(solution)/shard_map/inverse_factor/pallas_call | solution.py:127
  386.3 0.0 copy-start.2
  386.3 2.1 copy-done.2
  388.4 60.8 %reduce-scatter.4.cloned.1.call-done = f32[448,1024]{1,0:T(8,128)} async-done(((f32[1792,1024]{1,0:T(8,128)}), f32[448,1024]{1,0:T(8,128)}) %reduce-scatter.4.cloned.1.call-update) | async-done | bytes 1835024
  449.3 0.0 copy-start.3
  449.3 0.0 copy-start.1
  449.3 5.9 %fusion.7 = f32[448,1024]{1,0:T(8,128)S(1)} fusion(f32[448,1024]{1,0:T(8,128)} %reduce-scatter.4.cloned.1.call-done, f32[1024,1024]{1,0:T(8,128)} %copy-done.2), kind=kOutput, calls=%fused_computation.10 | convolution fusion | flops 2818572288 | bytes 7864320 | tf_op jit(solution)/shard_map/dot_general | solution.py:168
  455.2 0.0 copy-done.3
  455.2 4.6 fusion.8
  459.8 0.0 copy-done.1
Async XLA Ops:
  6.5 1.2 copy-start
  6.5 60.4 %all-reduce.4.cloned.1.call-start = ((), (), s32[]{:S(2)}) async-start(), calls=%async_computation.1 | async-start | bytes 2097152 | tf_op jit(solution)/shard_map/psum | solution.py:148
  12.2 142.3 %all-reduce.6.cloned.1.call-start = ((), (), s32[]{:S(2)}) async-start(), calls=%async_computation.2 | async-start | bytes 8388608 | tf_op jit(solution)/shard_map/psum | solution.py:150
  66.9 7.2 %copy-start.5 = (f32[256,1024]{1,0:T(8,128)S(1)}, f32[256,1024]{1,0:T(8,128)}, u32[]{:S(2)}) copy-start(f32[256,1024]{1,0:T(8,128)} %all-reduce.4.cloned.1.call-done) | copy-start | bytes 3145732
  74.0 210.7 %all-reduce.8.cloned.1.call-start = ((), (), s32[]{:S(2)}) async-start(), calls=%async_computation.3 | async-start | bytes 16777216 | tf_op jit(solution)/shard_map/psum | solution.py:157
  154.6 294.7 %reduce-scatter.4.cloned.1.call-start = ((), (), s32[]{:S(2)}) async-start(), calls=%async_computation.4 | async-start | bytes 9175040
  284.7 14.3 %copy-start.6 = (f32[2048,1024]{0,1:T(8,128)S(1)}, f32[2048,1024]{0,1:T(8,128)}, u32[]{:S(2)}) copy-start(f32[2048,1024]{0,1:T(8,128)} %all-reduce.8.cloned.1.call-done) | copy-start | bytes 25165828
  321.2 2.2 copy-start.4
  386.3 2.1 copy-start.2
  449.3 5.9 %copy-start.3 = (f32[1024,1024]{1,0:T(8,128)S(1)}, f32[1024,1024]{1,0:T(8,128)}, u32[]{:S(2)}) copy-start(f32[1024,1024]{1,0:T(8,128)} %copy-done.2) | copy-start | bytes 12582916
  449.3 10.5 %copy-start.1 = (bf16[256,2048]{1,0:T(8,128)(2,1)S(1)}, bf16[256,2048]{1,0:T(8,128)(2,1)}, u32[]{:S(2)}) copy-start(bf16[256,2048]{1,0:T(8,128)(2,1)} %param.3) | copy-start | bytes 3145732
Sparse Core Ops, SparseCore 0:
  12.3 54.5 all-reduce.3
  74.1 80.3 all-reduce.5
  158.0 126.6 all-reduce.7
  321.3 127.9 reduce-scatter.3

commit v2 on v1

--- a/solution.py
+++ b/solution.py
@@ -1,3 +1,6 @@
+import functools
+import math
+
 import jax
 import jax.numpy as jnp
 from jax import lax
@@ -135,45 +138,216 @@
         ],
         compiler_params=pltpu.CompilerParams(vmem_limit_bytes=32 * 1024 * 1024),
         cost_estimate=pl.CostEstimate(
-            flops=100_000_000_000, bytes_accessed=8 * n * n, transcendentals=0
+            flops=10_000_000_000, bytes_accessed=8 * n * n, transcendentals=0
         ),
         name="inverse_factor",
     )(gram)
 
 
-def shards(activations, weight, basis):
+def all_reduce_kernel(axis, size, parts, x_ref, out_ref, acc, *rest):
+    bits = size.bit_length() - 1
+    land, (send, recv) = rest[:bits], rest[bits:]
+    rows = x_ref.shape[0] // parts
+    me = lax.axis_index(axis)
+    bit = [lax.rem(me // (1 << b), 2) for b in range(bits)]
+    peer = [me + (1 - 2 * bit[b]) * (1 << b) for b in range(bits)]
+
+    barrier = pltpu.get_barrier_semaphore()
+    for b in range(bits):
+        pl.semaphore_signal(
+            barrier, inc=1, device_id={axis: peer[b]}, device_id_type=pl.DeviceIdType.MESH
+        )
+    pl.semaphore_wait(barrier, bits)
+
+    orders = []
+    for p in range(parts):
+        order = list(range(bits))
+        if p % 2:
+            order[-2:] = order[-2:][::-1]
+        orders.append(order)
+    starts = [[p * rows + jnp.int32(0)] for p in range(parts)]
+    for p in range(parts):
+        for s in range(bits):
+            starts[p].append(starts[p][-1] + bit[orders[p][s]] * (rows >> (s + 1)))
+
+    def copy(src, dst, p, s, phase):
+        return pltpu.make_async_remote_copy(
+            src_ref=src,
+            dst_ref=dst,
+            send_sem=send.at[phase, p, s],
+            recv_sem=recv.at[phase, p, s],
+            device_id={axis: peer[orders[p][s]]},
+            device_id_type=pl.DeviceIdType.MESH,
+        )
+
+    def region(start, length):
+        return pl.ds(pl.multiple_of(start, 8), length)
+
+    def halve(p, s):
+        length = rows >> (s + 1)
+        away = starts[p][s] + (1 - bit[orders[p][s]]) * length
+        src = x_ref if s == 0 else acc
+        c = copy(src.at[region(away, length)], land[s].at[pl.ds(p * length, length)], p, s, 0)
+        c.start()
+        return c
+
+    def add(p, s):
+        length = rows >> (s + 1)
+        src = x_ref if s == 0 else acc
+        dst = out_ref if s == bits - 1 else acc
+        chunk = min(length, 32)
+
+        def body(i, carry):
+            own = region(starts[p][s + 1] + i * chunk, chunk)
+            dst[own] = src[own] + land[s][region(p * length + i * chunk, chunk)]
+            return carry
+
+        lax.fori_loop(0, length // chunk, body, 0)
+
+    def double(p, s):
+        own = region(starts[p][s + 1], rows >> (s + 1))
+        c = copy(out_ref.at[own], out_ref.at[own], p, s, 1)
+        c.start()
+        return c
+
+    started = []
+    flying = [halve(p, 0) for p in range(parts)]
+    for s in range(bits):
+        for p in range(parts):
+            flying[p].wait_recv()
+            add(p, s)
+            started.append(flying[p])
+            flying[p] = halve(p, s + 1) if s + 1 < bits else double(p, s)
+    for s in range(bits - 1, -1, -1):
+        for p in range(parts):
+            flying[p].wait_recv()
+            started.append(flying[p])
+            if s:
+                flying[p] = double(p, s - 1)
+    for c in started:
+        c.wait_send()
+
+
+def all_reduce(x, axis, size, parts, collective_id):
+    bits = size.bit_length() - 1
+    rows, cols = x.shape
+    scratch = [pltpu.VMEM((rows, cols), jnp.float32)]
+    scratch += [pltpu.VMEM((rows >> (s + 1), cols), jnp.float32) for s in range(bits)]
+    scratch += [pltpu.SemaphoreType.DMA((2, parts, bits))] * 2
+    return pl.pallas_call(
+        functools.partial(all_reduce_kernel, axis, size, parts),
+        out_shape=jax.ShapeDtypeStruct((rows, cols), jnp.float32),
+        in_specs=[pl.BlockSpec(memory_space=pltpu.VMEM)],
+        out_specs=pl.BlockSpec(memory_space=pltpu.VMEM),
+        scratch_shapes=scratch,
+        compiler_params=pltpu.CompilerParams(
+            collective_id=collective_id,
+            has_side_effects=True,
+            vmem_limit_bytes=16 * rows * cols + 4 * 1024 * 1024,
+        ),
+        cost_estimate=pl.CostEstimate(
+            flops=rows * cols * 20_000, bytes_accessed=8 * rows * cols, transcendentals=0
+        ),
+        name="all_reduce_" + str(collective_id),
+    )(x)
+
+
+def cross_kernel(weight_ref, moments_ref, out_ref, high, rest):
+    depth = moments_ref.shape[0]
+    chunk = 128
+
+    @pl.when(pl.program_id(0) == 0)
+    def _():
+        def body(i, carry):
+            s = pl.ds(pl.multiple_of(i * chunk, chunk), chunk)
+            value = moments_ref[s]
+            top = value.astype(jnp.bfloat16)
+            high[s] = top
+            rest[s] = (value - top.astype(jnp.float32)).astype(jnp.bfloat16)
+            return carry
+
+        lax.fori_loop(0, depth // chunk, body, 0)
+
+    rows = weight_ref[...]
+    out_ref[...] = jnp.dot(rows, high[...], preferred_element_type=jnp.float32) + jnp.dot(
+        rows, rest[...], preferred_element_type=jnp.float32
+    )
+
+
+def cross_product(weight, moments):
+    rows, depth = weight.shape
+    cols = moments.shape[1]
+    tile = math.gcd(rows, 256)
+    return pl.pallas_call(
+        cross_kernel,
+        grid=(rows // tile,),
+        out_shape=jax.ShapeDtypeStruct((rows, cols), jnp.float32),
+        in_specs=[
+            pl.BlockSpec((tile, depth), lambda i: (i, 0)),
+            pl.BlockSpec((depth, cols), lambda i: (0, 0)),
+        ],
+        out_specs=pl.BlockSpec((tile, cols), lambda i: (i, 0)),
+        scratch_shapes=[pltpu.VMEM((depth, cols), jnp.bfloat16)] * 2,
+        compiler_params=pltpu.CompilerParams(vmem_limit_bytes=24 * 1024 * 1024),
+        cost_estimate=pl.CostEstimate(
+            flops=4 * rows * depth * cols,
+            bytes_accessed=2 * rows * depth + 4 * cols * (rows + depth),
+            transcendentals=0,
+        ),
+        name="cross_product",
+    )(weight, moments)
+
+
+def shards(mesh, activations, weight, basis):
+    tok, ch = mesh.shape["tok"], mesh.shape["ch"]
     partial_value = lax.dot_general(
         activations, basis, (((1,), (1,)), ((), ())), preferred_element_type=jnp.float32
     )
-    codes = lax.psum(partial_value, "ch")
+    codes = all_reduce(partial_value, "ch", ch, 2, 1)
+    codes_low = codes.astype(jnp.bfloat16)
+    half = codes.shape[1] // 2
+
+    def moments_of(c):
+        return lax.dot_general(
+            activations,
+            codes_low[:, c * half : (c + 1) * half],
+            (((0,), (0,)), ((), ())),
+            preferred_element_type=jnp.float32,
+        )
+
+    def cross_of(moments):
+        return cross_product(weight, moments)
+
+    def scatter(part):
+        return lax.psum_scatter(part, "ch", scatter_dimension=0, tiled=True)
+
+    first = cross_of(all_reduce(moments_of(0), "tok", tok, 4, 2))
+    first, local = lax.optimization_barrier((first, moments_of(1)))
+    cross_first = scatter(first)
+    second = cross_of(all_reduce(local, "tok", tok, 4, 2))
     local_gram = dot_f32(codes, codes, (((0,), (0,)), ((), ())))
-    gram = lax.psum(local_gram, "tok")
-    codes_low = codes.astype(jnp.bfloat16)
-    local_moments = lax.dot_general(
-        activations, codes_low, (((0,), (0,)), ((), ())), preferred_element_type=jnp.float32
-    )
-    gram, local_moments = lax.optimization_barrier((gram, local_moments))
-    inverse = inverse_factor(gram)
-    moments = lax.psum(local_moments, "tok")
-    high = lax.reduce_precision(moments, 8, 7)
-    rest = (moments - high).astype(jnp.bfloat16)
-    high = high.astype(jnp.bfloat16)
-    cross = lax.psum_scatter(
-        jnp.dot(weight, high, preferred_element_type=jnp.float32)
-        + jnp.dot(weight, rest, preferred_element_type=jnp.float32),
-        "ch",
-        scatter_dimension=0,
-        tiled=True,
-    )
-    middle = lax.dot_general(
-        cross, inverse, NT, precision=lax.Precision.HIGH, preferred_element_type=jnp.float32
-    )
-    return jnp.dot(
-        middle, inverse, precision=lax.Precision.HIGH, preferred_element_type=jnp.float32
-    )
+    second, local_gram, cross_first = lax.optimization_barrier((second, local_gram, cross_first))
+    cross_second = scatter(second)
+    inverse = inverse_factor(all_reduce(local_gram, "tok", tok, 4, 3))
+
+    def high_dot(a, b, dims):
+        return lax.dot_general(
+            a, b, dims, precision=lax.Precision.HIGH, preferred_element_type=jnp.float32
+        )
+
+    middle = high_dot(cross_first, inverse[:, :half], NT) + high_dot(
+        cross_second, inverse[:, half:], NT
+    )
+    return high_dot(middle, inverse, (((1,), (0,)), ((), ())))
 
 
 def solution(mesh):
     in_specs = (P("tok", "ch"), P("tok", "ch"), P(None, "ch"))
     out_specs = P(("tok", "ch"), None)
-    return jax.shard_map(shards, mesh=mesh, in_specs=in_specs, out_specs=out_specs, check_vma=False)
+    return jax.shard_map(
+        functools.partial(shards, mesh),
+        mesh=mesh,
+        in_specs=in_specs,
+        out_specs=out_specs,
+        check_vma=False,
+    )

time: 472 us -> 305 us (0.65); the launches traced: 467 us -> 305 us
  waiting for transfers between devices: 321 us -> 9.59 us
  Pallas kernels: 63 us -> 250 us
  matrix products: 54.6 us -> 22 us
  local copies, waits for them, and re-layouts: 13.9 us -> 8.97 us
    psum x3 -> x0, waiting for transfers between devices: 261 us -> none  [the longest x1 130 us: shards(): moments = lax.psum(local_moments, 'tok')]
    pallas_call x0 -> x6, Pallas kernels: none -> 187 us  [the longest x4 168 us: all_reduce(): pl.pallas_call(functools.partial(all_reduce_kernel, axis, size, parts), o...]
    unnamed x5 -> x2, waiting for transfers between devices: 60.9 us -> 0.03 us
    dot_general x5, matrix products: 43.1 us -> 13.5 us  [the longest x3 9.99 us: high_dot(): lax.dot_general(a, b, dims, precision=lax.Precision.HIGH, preferred_eleme...]
    reduce_scatter x0 -> x2, waiting for transfers between devices: none -> 9.56 us  [scatter(): return lax.psum_scatter(part, 'ch', scatter_dimension=0, tiled=True)]
    unnamed x15 -> x24, local copies, waits for them, and re-layouts: 13.9 us -> 8.97 us
  transfers between devices with their start and end apart: 4 -> 2, of which waited for: 4 -> 1; matrix products, arithmetic and copies ran while one was open for 1% -> 2% of each run, Pallas kernels for 13% -> 51%
where the time goes in v2:
time: 305 us
  Pallas kernels  250 us (82%)
  matrix products  22 us (7%)
  between operations  13.6 us (4%)
  waiting for transfers between devices  9.59 us (3%)
  local copies, waits for them, and re-layouts  8.97 us (3%)
    pallas_call x4, Pallas kernels, all_reduce(): pl.pallas_call(functools.partial(all_reduce_kernel, axis, size, parts), o...  168 us
    pallas_call x1, Pallas kernels, inverse_factor(): pl.pallas_call(inverse_factor_kernel, out_shape=jax.ShapeDtypeStruct((n,...  62.9 us
    pallas_call x2, Pallas kernels, cross_product(): pl.pallas_call(cross_kernel, grid=(rows // tile,), out_shape=jax.ShapeDty...  18.9 us
    dot_general x3, matrix products, high_dot(): lax.dot_general(a, b, dims, precision=lax.Precision.HIGH, preferred_eleme...  9.99 us
    reduce_scatter x2, waiting for transfers between devices, scatter(): return lax.psum_scatter(part, 'ch', scatter_dimension=0, tiled=True)  9.56 us
    unnamed x24, local copies, waits for them, and re-layouts  8.97 us
  transfers between devices with their start and end apart: 2, of which 1 were waited for; matrix products, arithmetic and copies ran while one was open for 2% of the time, Pallas kernels for 51%

profile of v2, /device:TPU:0, one launch (start us, length us, event | category | flops | bytes accessed | tf_op | source)
XLA Modules:
  0.0 304.5 jit_solution(6605121844096607504)
XLA Ops:
  6.5 0.0 copy-start
  6.5 0.0 reduce-scatter.3.cloned.1.call-start
  6.5 1.2 copy-done
  7.8 3.5 %fusion.8.x_ref = f32[256,1024]{1,0:T(8,128)S(1)} fusion(bf16[256,2048]{1,0:T(8,128)(2,1)S(1)} %copy-done, bf16[1024,2048]{1,0:T(8,128)(2,1)} %param.5), kind=kOutput, calls=%fused_computation.10 | convolution fusion | flops 1073741824 | bytes 6291456 | tf_op jit(solution)/shard_map/dot_general | solution.py:303
  11.2 43.4 %all_reduce_1.1 = f32[256,1024]{1,0:T(8,128)S(1)} custom-call(f32[256,1024]{1,0:T(8,128)S(1)} %fusion.8.x_ref), custom_call_target="tpu_custom_call" | custom-call | flops 5242880000 | bytes 2097152 | tf_op jit(solution)/shard_map/all_reduce_1/pallas_call | solution.py:237
  54.7 0.1 convert_element_type.3
  54.8 0.8 convolution_bitcast_fusion.1.x_ref
  55.5 0.0 slice-start
  55.5 2.7 convolution_bitcast_fusion.x_ref
  58.3 0.0 slice-start.1
  58.3 41.6 %all_reduce_2.2.moments_ref = f32[2048,512]{1,0:T(8,128)S(1)} custom-call(f32[2048,512]{1,0:T(8,128)S(1)} %convolution_bitcast_fusion.1.x_ref), custom_call_target="tpu_custom_call" | custom-call | flops 20971520000 | bytes 8388608 | tf_op jit(solution)/shard_map/all_reduce_2/pallas_call | solution.py:237
  99.9 0.0 slice-done
  99.9 0.0 slice-done.1
  99.9 9.5 %cross_product.2 = f32[1792,512]{1,0:T(8,128)S(1)} custom-call(bf16[1792,2048]{1,0:T(8,128)(2,1)S(1)} %bitcast.14, f32[2048,512]{1,0:T(8,128)S(1)} %all_reduce_2.2.moments_ref), custom_call_target="tpu_custom_call" | custom-call | flops 7516192768 | bytes 15204352 | tf_op jit(solution)/shard_map/cross_product/pallas_call | solution.py:281
  109.4 0.0 copy-start.5
  109.4 1.8 copy-done.5
  111.2 0.0 reduce-scatter.3.cloned.1.call-update
  111.2 0.0 reduce-scatter.5.cloned.1.call-start
  111.3 0.0 copy-start.4
  111.3 0.0 slice-start.2
  111.3 5.1 %fusion.9.x_ref = f32[1024,1024]{1,0:T(8,128)} fusion(f32[256,1024]{1,0:T(8,128)S(1)} %all_reduce_1.1), kind=kOutput, calls=%fused_computation.11 | convolution fusion | flops 3221225472 | bytes 5242880 | tf_op jit(solution)/shard_map/dot_general | solution.py:18
  116.4 0.0 copy-done.4
  116.4 0.0 slice-start.3
  116.4 41.4 %all_reduce_2.3.moments_ref = f32[2048,512]{1,0:T(8,128)S(1)} custom-call(f32[2048,512]{1,0:T(8,128)S(1)} %copy-done.4), custom_call_target="tpu_custom_call" | custom-call | flops 20971520000 | bytes 8388608 | tf_op jit(solution)/shard_map/all_reduce_2/pallas_call | solution.py:237
  157.8 0.0 slice-done.2
  157.8 0.0 slice-done.3
  157.8 9.5 %cross_product.3 = f32[1792,512]{1,0:T(8,128)S(1)} custom-call(bf16[1792,2048]{1,0:T(8,128)(2,1)S(1)} %bitcast.16, f32[2048,512]{1,0:T(8,128)S(1)} %all_reduce_2.3.moments_ref), custom_call_target="tpu_custom_call" | custom-call | flops 7516192768 | bytes 15204352 | tf_op jit(solution)/shard_map/cross_product/pallas_call | solution.py:281
  167.3 0.0 copy-start.6
  167.3 1.8 copy-done.6
  169.1 9.5 %reduce-scatter.3.cloned.1.call-done = f32[448,512]{1,0:T(8,128)} async-done(((f32[1792,512]{1,0:T(8,128)}), f32[448,512]{1,0:T(8,128)}) %reduce-scatter.3.cloned.1.call-update) | async-done | bytes 917520 | tf_op jit(solution)/shard_map/reduce_scatter | solution.py:322
  178.6 0.0 reduce-scatter.5.cloned.1.call-update
  178.7 0.0 copy-start.3
  178.7 2.2 copy-done.3
  180.8 41.9 %all_reduce_3.1.gram_ref = f32[1024,1024]{1,0:T(8,128)S(1)} custom-call(f32[1024,1024]{1,0:T(8,128)S(1)} %copy-done.3), custom_call_target="tpu_custom_call" | custom-call | flops 20971520000 | bytes 8388608 | tf_op jit(solution)/shard_map/all_reduce_3/pallas_call | solution.py:237
  222.7 0.0 copy-start.7
  222.7 62.9 %inverse_factor.1 = f32[1024,1024]{1,0:T(8,128)S(1)} custom-call(f32[1024,1024]{1,0:T(8,128)S(1)} %all_reduce_3.1.gram_ref), custom_call_target="tpu_custom_call" | custom-call | flops 10000000000 | bytes 8388608 | tf_op jit(solution)/shard_map/inverse_factor/pallas_call | solution.py:130
  285.6 0.0 copy-start.1
  285.7 2.0 copy-done.1
  287.6 0.0 copy-done.7
  287.6 1.7 fusion.2
  289.3 0.0 reduce-scatter.5.cloned.1.call-done
  289.3 0.0 copy-start.2
  289.3 3.7 %fusion = f32[448,1024]{1,0:T(8,128)S(1)} fusion(f32[448,512]{1,0:T(8,128)} %reduce-scatter.5.cloned.1.call-done, f32[1024,1024]{1,0:T(8,128)} %copy-done.1), kind=kOutput, calls=%fused_computation.2 | convolution fusion | flops 1409286144 | bytes 4849664 | tf_op jit(solution)/shard_map/dot_general | solution.py:334
  293.0 0.0 copy-done.2
  293.0 4.6 %fusion.4 = f32[448,1024]{1,0:T(8,128)} fusion(f32[1024,1024]{1,0:T(8,128)S(1)} %copy-done.2, f32[448,1024]{1,0:T(8,128)S(1)} %fusion.2, f32[448,1024]{1,0:T(8,128)S(1)} %fusion), kind=kOutput, calls=%fused_computation.6 | convolution fusion | flops 2819031040 | bytes 9699328 | tf_op jit(solution)/shard_map/dot_general | solution.py:334
  (2 shorter events, 0.0 us)
Async XLA Ops:
  6.5 1.2 copy-start
  6.5 172.1 %reduce-scatter.3.cloned.1.call-start = ((), (), s32[]{:S(2)}) async-start(), calls=%async_computation.2 | async-start | bytes 4587520 | tf_op jit(solution)/shard_map/reduce_scatter | solution.py:322
  55.5 44.4 %slice-start = ((s8[7340032]{0:T(1024)(128)(4,1)}), s8[4194304]{0:T(1024)(128)(4,1)S(1)}, s32[]{:S(2)}) async-start(s8[7340032]{0:T(1024)(128)(4,1)} %bitcast.13), calls=%async_computation.4 | async-start | bytes 8388608
  58.3 41.6 %slice-start.1 = ((s8[7340032]{0:T(1024)(128)(4,1)}), s8[3145728]{0:T(1024)(128)(4,1)S(1)}, s32[]{:S(2)}) async-start(s8[7340032]{0:T(1024)(128)(4,1)} %bitcast.13), calls=%async_computation.5 | async-start | bytes 6291456
  109.4 1.8 copy-start.5
  111.2 178.1 %reduce-scatter.5.cloned.1.call-start = ((), (), s32[]{:S(2)}) async-start(), calls=%async_computation.3 | async-start | bytes 4587520 | tf_op jit(solution)/shard_map/reduce_scatter | solution.py:322
  111.3 5.1 %copy-start.4 = (f32[2048,512]{1,0:T(8,128)S(1)}, f32[2048,512]{1,0:T(8,128)}, u32[]{:S(2)}) copy-start(f32[2048,512]{1,0:T(8,128)} %convolution_bitcast_fusion.x_ref) | copy-start | bytes 12582916
  111.3 46.5 %slice-start.2 = ((s8[7340032]{0:T(1024)(128)(4,1)}), s8[4194304]{0:T(1024)(128)(4,1)S(1)}, s32[]{:S(2)}) async-start(s8[7340032]{0:T(1024)(128)(4,1)} %bitcast.15), calls=%async_computation.6 | async-start | bytes 8388608
  116.4 41.5 %slice-start.3 = ((s8[7340032]{0:T(1024)(128)(4,1)}), s8[3145728]{0:T(1024)(128)(4,1)S(1)}, s32[]{:S(2)}) async-start(s8[7340032]{0:T(1024)(128)(4,1)} %bitcast.15), calls=%async_computation.7 | async-start | bytes 6291456
  167.3 1.8 copy-start.6
  178.7 2.2 copy-start.3
  222.7 64.9 %copy-start.7 = (f32[448,512]{1,0:T(8,128)S(1)}, f32[448,512]{1,0:T(8,128)}, u32[]{:S(2)}) copy-start(f32[448,512]{1,0:T(8,128)} %reduce-scatter.3.cloned.1.call-done) | copy-start | bytes 2752516
  285.6 2.0 copy-start.1
  289.3 3.7 %copy-start.2 = (f32[1024,1024]{1,0:T(8,128)S(1)}, f32[1024,1024]{1,0:T(8,128)}, u32[]{:S(2)}) copy-start(f32[1024,1024]{1,0:T(8,128)} %copy-done.1) | copy-start | bytes 12582916
Sparse Core Ops, SparseCore 0:
  111.3 67.2 reduce-scatter.2
  180.9 68.7 reduce-scatter.4
